TPU v7x, 32 devices: a whole 2x2x4 slice. The times are simulated.
32 devices in a mesh: fsdp: 8 (over z, y), seq: 4 (over x, core).
Axes of the slice: x: 2, y: 2, z: 4, core: 2. Of those that a mesh axis runs over, the one named last changes fastest.
Arguments:
- text_embeds: bfloat16 [2240, 4096], P('fsdp'), may hold values from -8 to 8
- vision_tokens: bfloat16 [1024, 4096], P('fsdp', 'seq'), may hold values from -6 to 6
- vision_request: int32 [1024, 1], P('fsdp'), may hold values from 0 to 7; in each aligned block of 128 rows (0 to 127, 128 to 255, ...) at most 32 rows name the same one
- image_start: int32 [8], P('fsdp'), may hold values from 1 to 16
- lengths: int32 [8], P('fsdp'), may hold values from 273 to 280
- attn_gain: float32 [4096], replicated, may hold values from 0.5 to 1.5
- w_query: bfloat16 [4096, 2048], P('fsdp', 'seq'), may hold values from -1 to 1
- w_key: bfloat16 [4096, 2048], P('fsdp', 'seq'), may hold values from -1 to 1
- w_value: bfloat16 [4096, 2048], P('fsdp', 'seq'), may hold values from -0.09375 to 0.09375
- w_out: bfloat16 [2048, 4096], P(None, 'fsdp'), may hold values from -0.125 to 0.125
- final_gain: float32 [4096], replicated, may hold values from 0.25 to 1.75
- lm_head: bfloat16 [4096, 32000], P(None, 'fsdp'), may hold values from -0.25 to 0.25
Outputs:
- state_rms: float32 [8], P('seq')
- max_logit: float32 [8], P('seq')
Inputs may be any that keep to these rules, and one draw needn't show every extreme that they name: `vision_request`: within the 128 vision tokens of one index of fsdp no request is named more than 32 times, a bound that some block reaches; every request is named by some vision token. `lengths`: each request's image tokens end before its last token.
All inputs are finite; a program needn't handle non-finite values.
Results may differ from a plain program's by a relative error of at most 0.0024.
Values may be sent and summed in bfloat16 or wider, within the bound.
A program may use at most 128 MiB of HBM per device.

v0:
```python
import math

import jax
import jax.numpy as jnp
from jax import lax
from jax.sharding import PartitionSpec as P

HD = 128


norm_epsilon = 1e-05


def row_norm(rows, gain):
    widened = rows.astype(jnp.float32)
    return (
        widened
        * lax.rsqrt(jnp.mean(widened * widened, axis=1, keepdims=True) + norm_epsilon)
        * gain
    ).astype(jnp.bfloat16)


def pack_slots(tokens, destination, slot_index, groups, capacity):
    return (
        jnp.zeros((groups, capacity, tokens.shape[1]), jnp.bfloat16)
        .at[destination, slot_index]
        .set(tokens)
    )


def local(
    text_embeds,
    vision_tokens,
    vision_request,
    image_start,
    lengths,
    attn_gain,
    w_query,
    w_key,
    w_value,
    w_out,
    final_gain,
    lm_head,
):
    groups = lax.axis_size("fsdp")
    seq_count = lax.axis_size("seq")
    group_index = lax.axis_index("fsdp")
    seq_index = lax.axis_index("seq")
    seq_len = text_embeds.shape[0]
    width = text_embeds.shape[1]
    columns = w_key.shape[1]
    dpiece = width // groups
    quarter = groups // seq_count
    capacity = max(2, 2 * vision_tokens.shape[0] // groups)
    last_index = lengths[0] - 1
    final_text = lax.dynamic_slice_in_dim(text_embeds, last_index, 1, 0)
    text_pieces = final_text.reshape(groups, dpiece)
    destination = vision_request[:, 0]
    onehot = (destination[:, None] == jnp.arange(groups, dtype=jnp.int32)[None, :]).astype(
        jnp.int32
    )
    slot_index = jnp.sum((jnp.cumsum(onehot, axis=0) - onehot) * onehot, axis=1)
    counts = jnp.sum(onehot, axis=0)
    full_vision = lax.all_gather(vision_tokens, "seq", axis=1, tiled=True)
    outbox = pack_slots(full_vision, destination, slot_index, groups, capacity)
    received, arrived, text_part = (
        lax.all_to_all(outbox, "fsdp", split_axis=0, concat_axis=0, tiled=True),
        lax.all_to_all(counts[:, None], "fsdp", split_axis=0, concat_axis=0, tiled=True),
        lax.all_to_all(text_pieces, "fsdp", split_axis=0, concat_axis=0, tiled=True),
    )
    occupied = (
        (jnp.arange(capacity, dtype=jnp.int32)[None, :] < arrived).astype(jnp.int32).reshape(-1)
    )
    ranking = jnp.cumsum(occupied) - occupied
    positions = jnp.where(occupied > 0, image_start[0] + ranking, seq_len)
    states = text_embeds.at[positions].set(received.reshape(-1, width), mode="drop")
    normed = row_norm(states, attn_gain)
    last_row = lax.dynamic_slice_in_dim(normed, last_index, 1, 0)
    query_sum = jnp.dot(
        last_row,
        lax.all_gather(w_query, "fsdp", axis=0, tiled=True),
        preferred_element_type=jnp.float32,
    )
    key_sum = jnp.dot(
        normed,
        lax.all_gather(w_key, "fsdp", axis=0, tiled=True),
        preferred_element_type=jnp.float32,
    )
    value_sum = jnp.dot(
        normed,
        lax.all_gather(w_value, "fsdp", axis=0, tiled=True),
        preferred_element_type=jnp.float32,
    )
    heads_local = columns // HD
    query_heads = query_sum.astype(jnp.bfloat16).reshape(heads_local, HD)
    key_heads = key_sum.astype(jnp.bfloat16).reshape(seq_len, heads_local, HD)
    value_heads = value_sum.astype(jnp.bfloat16).reshape(seq_len, heads_local, HD)
    scores = jnp.einsum(
        "hc,jhc->hj", query_heads, key_heads, preferred_element_type=jnp.float32
    ) / math.sqrt(HD)
    live_keys = jnp.arange(seq_len, dtype=jnp.int32) < lengths[0]
    scores = jnp.where(live_keys[None, :], scores, -jnp.inf)
    peak = jnp.max(scores, axis=1, keepdims=True)
    shifted = jnp.exp(scores - peak)
    weights = (shifted / jnp.sum(shifted, axis=1, keepdims=True)).astype(jnp.bfloat16)
    attended = (
        jnp.einsum("hj,jhc->hc", weights, value_heads, preferred_element_type=jnp.float32)
        .astype(jnp.bfloat16)
        .reshape(1, columns)
    )
    gathered = lax.all_gather(attended, ("fsdp", "seq"), axis=0, tiled=True)
    attended_all = gathered.reshape(groups, seq_count * columns)
    attended_mine = lax.dynamic_slice_in_dim(attended_all, seq_index * quarter, quarter, 0)
    text_mine = lax.dynamic_slice_in_dim(text_part, seq_index * quarter, quarter, 0)
    residual_out = text_mine.astype(jnp.float32) + jnp.dot(
        attended_mine, w_out, preferred_element_type=jnp.float32
    )
    gain_part = lax.dynamic_slice_in_dim(final_gain, group_index * dpiece, dpiece, 0)
    scaled_out = (residual_out * gain_part[None, :]).astype(jnp.bfloat16)
    square_part = jnp.sum(residual_out * residual_out, axis=1)[None, :]
    full_scaled, square_parts = (
        lax.all_gather(scaled_out, "fsdp", axis=1, tiled=True),
        lax.all_gather(square_part.astype(jnp.bfloat16), "fsdp", axis=0, tiled=True).astype(
            square_part.dtype
        ),
    )
    mean_square = jnp.sum(square_parts, axis=0) / width
    logits = jnp.dot(full_scaled, lm_head, preferred_element_type=jnp.float32)
    local_max = jnp.max(logits, axis=1) * lax.rsqrt(mean_square + norm_epsilon)
    max_logit = lax.pmax(local_max, "fsdp")
    return (jnp.sqrt(mean_square), max_logit)


def solution(mesh):
    return jax.shard_map(
        local,
        mesh=mesh,
        in_specs=(
            P("fsdp", None),
            P("fsdp", "seq"),
            P("fsdp", None),
            P("fsdp"),
            P("fsdp"),
            P(),
            P("fsdp", "seq"),
            P("fsdp", "seq"),
            P("fsdp", "seq"),
            P(None, "fsdp"),
            P(),
            P(None, "fsdp"),
        ),
        out_specs=(P("seq"), P("seq")),
        check_vma=False,
    )
```

profile of v0, /device:TPU:0, one launch (start us, length us, event | category | flops | bytes accessed | tf_op | source)
XLA Modules:
  0.0 417.0 jit_solution(4008045209098227903)
XLA Ops:
  7.2 3.4 copy.57
  10.7 0.7 all-gather.9.cloned.1.call-update
  11.5 0.7 all-gather.11.cloned.1.call-update
  12.6 0.7 copy.19
  13.3 7.3 %all-to-all-start.1 = ((s32[8,1,1]{2,1,0:T(1,128)}), s32[8,1,1]{2,1,0:T(1,128)S(1)}, u32[]{:S(2)}, u32[]{:S(2)}) async-start(s32[8,1,1]{2,1,0:T(1,128)} %copy.19), calls=%async_computation.1 | async-start | bytes 8192 | tf_op jit(solution)/shard_map/all_to_all | solution.py:68
  20.6 0.5 all-gather.13.cloned.1.call-update
  21.8 0.9 constant_dynamic-slice_fusion.1
  22.7 0.5 broadcast.134
  23.2 0.7 reduce.5
  23.9 0.6 reshape.204
  24.5 2.6 all-to-all-done.1
  27.1 3.4 all-to-all-start
  30.5 1.6 broadcast_in_dim.20
  32.1 33.9 %scatter_fusion = bf16[8,32,4096]{2,1,0:T(8,128)(2,1)} fusion(bf16[8,32,4096]{2,1,0:T(8,128)(2,1)} %broadcast_in_dim.20, s32[128]{0:T(128)S(1)} %fusion.27, bf16[128,4096]{1,0:T(8,128)(2,1)S(1)} %copy-done.2), kind=kCustom, calls=%fused_computation | custom fusion | bytes 3146752 | tf_op jit(solution)/shard_map/scatter | solution.py:27
  66.0 6.2 %all-to-all-start.2 = ((bf16[8,32,4096]{2,1,0:T(8,128)(2,1)}), bf16[8,32,4096]{2,1,0:T(8,128)(2,1)}, u32[]{:S(2)}, u32[]{:S(2)}) async-start(bf16[8,32,4096]{2,1,0:T(8,128)(2,1)} %scatter_fusion), calls=%async_computation.2 | async-start | bytes 4194304 | tf_op jit(solution)/shard_map/all_to_all | solution.py:67
  73.0 0.8 dynamic_slice.19
  73.7 0.6 dynamic-slice.1
  76.2 71.7 %all-to-all-done.2 = bf16[8,32,4096]{2,1,0:T(8,128)(2,1)} async-done(((bf16[8,32,4096]{2,1,0:T(8,128)(2,1)}), bf16[8,32,4096]{2,1,0:T(8,128)(2,1)}, u32[]{:S(2)}, u32[]{:S(2)}) %all-to-all-start.2) | async-done | bytes 2097184 | tf_op jit(solution)/shard_map/all_to_all | solution.py:67
  147.9 7.9 %scatter_fusion.1 = bf16[280,4096]{1,0:T(8,128)(2,1)} fusion(bf16[280,4096]{1,0:T(8,128)(2,1)} %copy.57, s32[256]{0:T(256)S(1)} %bitcast.66, bf16[256,4096]{1,0:T(8,128)(2,1)} %bitcast.10), kind=kCustom, calls=%fused_computation.1 | custom fusion | bytes 6292480 | tf_op jit(solution)/shard_map/scatter | solution.py:76
  155.8 2.3 fusion
  158.2 2.1 fusion.2
  160.3 2.9 fusion.13
  163.2 51.4 %all-gather.11.cloned.1.call-done = bf16[4096,512]{1,0:T(8,128)(2,1)} async-done(((bf16[512,512]{1,0:T(8,128)(2,1)}), bf16[4096,512]{1,0:T(8,128)(2,1)}) %all-gather.11.cloned.1.call-update) | async-done | bytes 4194320 | tf_op jit(solution)/shard_map/all_gather | solution.py:86
  214.6 4.2 %fusion.3 = bf16[35,4,8,128]{3,2,1,0:T(8,128)(2,1)S(1)} fusion(bf16[280,4096]{1,0:T(8,128)(2,1)} %fusion.2, bf16[4096,512]{1,0:T(8,128)(2,1)} %all-gather.11.cloned.1.call-done), kind=kOutput, calls=%fused_computation.9 | convolution fusion | flops 1174548480 | bytes 6774784 | tf_op jit(solution)/shard_map/dot_general | solution.py:84
  219.4 68.8 %all-gather.13.cloned.1.call-done = bf16[4096,512]{1,0:T(8,128)(2,1)} async-done(((bf16[512,512]{1,0:T(8,128)(2,1)}), bf16[4096,512]{1,0:T(8,128)(2,1)}) %all-gather.13.cloned.1.call-update) | async-done | bytes 4194320 | tf_op jit(solution)/shard_map/all_gather | solution.py:91
  288.3 4.2 %fusion.4 = bf16[35,4,8,128]{3,2,1,0:T(8,128)(2,1)S(1)} fusion(bf16[280,4096]{1,0:T(8,128)(2,1)} %fusion.2, bf16[4096,512]{1,0:T(8,128)(2,1)} %all-gather.13.cloned.1.call-done), kind=kOutput, calls=%fused_computation.10 | convolution fusion | flops 1174548480 | bytes 6774784 | tf_op jit(solution)/shard_map/dot_general | solution.py:89
  292.7 39.1 %all-gather.1 = bf16[32,1,512]{2,1,0:T(2,128)(2,1)S(1)} all-gather(bf16[1,1,512]{2,1,0:T(2,128)(2,1)S(1)} %reshape.187), channel_id=1, replica_groups=mesh['fsdp'=8,'seq'=4] {'fsdp','seq'}, dimensions={0}, use_global_device_ids=true | all-gather | bytes 33792 | tf_op jit(solution)/shard_map/all_gather | solution.py:111
  332.8 26.0 %all_gather.27 = bf16[2,4096]{1,0:T(2,128)(2,1)S(1)} all-gather(bf16[2,512]{1,0:T(2,128)(2,1)S(1)} %get-tuple-element.4), channel_id=1, replica_groups=mesh['fsdp'=8,'seq'=4] {'fsdp'}, dimensions={1}, use_global_device_ids=true | all-gather | bytes 18432 | tf_op jit(solution)/shard_map/all_gather | solution.py:122
  358.8 17.1 %all-reduce = bf16[16]{0:T(256)(128)(2,1)S(1)} all-reduce(bf16[16]{0:T(256)(128)(2,1)S(1)} %dynamic-update-slice), channel_id=2, replica_groups=mesh['fsdp'=8,'seq'=4] {'fsdp'}, use_global_device_ids=true, to_apply=%add | all-reduce | flops 16 | bytes 64
  376.0 14.3 %convolution_reduce_fusion = f32[2]{0:T(128)S(1)} fusion(bf16[2,4096]{1,0:T(2,128)(2,1)S(1)} %all_gather.27, bf16[4096,4000]{0,1:T(8,128)(2,1)} %param.23), kind=kOutput, calls=%fused_computation.11 | convolution fusion | flops 65544000 | bytes 32784392 | tf_op jit(solution)/shard_map/dot_general | solution.py:128
  390.3 0.5 rsqrt_multiply_fusion
  390.9 19.6 %pmax.7 = f32[2]{0:T(128)} all-reduce(f32[2]{0:T(128)S(1)} %get-tuple-element.6), channel_id=1, replica_groups=mesh['fsdp'=8,'seq'=4] {'fsdp'}, use_global_device_ids=true, to_apply=%region_13.14 | all-reduce | flops 2 | bytes 16 | tf_op jit(solution)/shard_map/pmax | solution.py:130
  (58 shorter events, 3.9 us)
Async XLA Ops:
  7.2 324.9 %copy-start = (bf16[2048,512]{1,0:T(8,128)(2,1)S(1)}, bf16[2048,512]{1,0:T(8,128)(2,1)}, u32[]{:S(2)}) copy-start(bf16[2048,512]{1,0:T(8,128)(2,1)} %param.21) | copy-start | bytes 6291460
  7.2 5.0 %copy-start.4 = (s32[128,1]{0,1:T(1,128)S(1)}, s32[128,1]{0,1:T(1,128)}, u32[]{:S(2)}) copy-start(s32[128,1]{0,1:T(1,128)} %param.14) | copy-start | bytes 1540
  7.2 23.3 %all-gather.7.cloned.1.call-start = ((), (), s32[]{:S(2)}) async-start(), calls=%async_computation.3 | async-start | bytes 1310720 | tf_op jit(solution)/shard_map/all_gather | solution.py:64
  10.7 149.6 %all-gather.9.cloned.1.call-start = ((), (), s32[]{:S(2)}) async-start(), calls=%async_computation.4 | async-start | bytes 4718592 | tf_op jit(solution)/shard_map/all_gather | solution.py:81
  11.4 203.2 %all-gather.11.cloned.1.call-start = ((), (), s32[]{:S(2)}) async-start(), calls=%async_computation.5 | async-start | bytes 4718592 | tf_op jit(solution)/shard_map/all_gather | solution.py:86
  13.3 13.7 %all-to-all-start.1 = ((s32[8,1,1]{2,1,0:T(1,128)}), s32[8,1,1]{2,1,0:T(1,128)S(1)}, u32[]{:S(2)}, u32[]{:S(2)}) async-start(s32[8,1,1]{2,1,0:T(1,128)} %copy.19), calls=%async_computation.1 | async-start | bytes 8192 | tf_op jit(solution)/shard_map/all_to_all | solution.py:68
  20.6 267.7 %all-gather.13.cloned.1.call-start = ((), (), s32[]{:S(2)}) async-start(), calls=%async_computation.6 | async-start | bytes 4718592 | tf_op jit(solution)/shard_map/all_gather | solution.py:91
  27.1 39.0 %all-to-all-start = ((bf16[8,2,256]{2,1,0:T(2,128)(2,1)}), bf16[8,2,256]{2,1,0:T(2,128)(2,1)S(1)}, u32[]{:S(2)}, u32[]{:S(2)}) async-start(bf16[8,2,256]{2,1,0:T(2,128)(2,1)} %reshape.204), calls=%async_computation | async-start | bytes 16384 | tf_op jit(solution)/shard_map/all_to_all | solution.py:69
  30.5 1.6 copy-start.2
  66.0 7.7 %copy-start.5 = (u32[32]{0:T(128)S(1)}, u32[32]{0:T(128)}, u32[]{:S(2)}) copy-start(u32[32]{0:T(128)} %constant.77) | copy-start | bytes 388
  66.0 81.8 %all-to-all-start.2 = ((bf16[8,32,4096]{2,1,0:T(8,128)(2,1)}), bf16[8,32,4096]{2,1,0:T(8,128)(2,1)}, u32[]{:S(2)}, u32[]{:S(2)}) async-start(bf16[8,32,4096]{2,1,0:T(8,128)(2,1)} %scatter_fusion), calls=%async_computation.2 | async-start | bytes 4194304 | tf_op jit(solution)/shard_map/all_to_all | solution.py:67
  147.9 10.3 %copy-start.3 = (f32[4096]{0:T(1024)S(1)}, f32[4096]{0:T(1024)}, u32[]{:S(2)}) copy-start(f32[4096]{0:T(1024)} %param.17) | copy-start | bytes 49156
  155.8 2.4 copy-start.1
Sparse Core Ops, SparseCore 0:
  10.8 19.4 all-gather.6
  32.4 107.5 all-gather.8
  142.1 72.4 all-gather.10
  216.6 71.6 all-gather.12
where the time goes:
time: 418 us; the launch traced here: 417 us
  waiting for transfers between devices  196 us (47%)
  blocking collectives  102 us (24%)
  local copies, waits for them, and re-layouts  51.9 us (12%)
  matrix products  26.5 us (6%)
  starting transfers between devices  17 us (4%)
  between operations  15.8 us (4%)
  other arithmetic  7.48 us (2%)
    all_to_all x1, waiting for transfers between devices, local(): lax.all_to_all(outbox, 'fsdp', split_axis=0, concat_axis=0, tiled=True)  71.7 us
    all_gather x1, waiting for transfers between devices, local(): lax.all_gather(w_value, 'fsdp', axis=0, tiled=True)  68.8 us
    all_gather x1, waiting for transfers between devices, local(): lax.all_gather(w_key, 'fsdp', axis=0, tiled=True)  51.4 us
    all_gather x1, blocking collectives, local(): gathered = lax.all_gather(attended, ('fsdp', 'seq'), axis=0, tiled=True)  39.1 us
    scatter x1, local copies, waits for them, and re-layouts, pack_slots(): return jnp.zeros((groups, capacity, tokens.shape[1]), jnp.bfloat16).at[de...  33.9 us
    all_gather x1, blocking collectives, local(): lax.all_gather(scaled_out, 'fsdp', axis=1, tiled=True)  26 us
    pmax x1, blocking collectives, local(): max_logit = lax.pmax(local_max, 'fsdp')  19.6 us
    unnamed x1, blocking collectives  17.1 us
  transfers between devices with their start and end apart: 7, of which 4 were waited for; matrix products, arithmetic and copies ran while one was open for 15% of the time, Pallas kernels for 0%

commit v1 on v0

v1 whole, which is shorter than its diff:
```python
import math

import jax
import jax.numpy as jnp
from jax import lax
from jax.sharding import PartitionSpec as P

HD = 128


norm_epsilon = 1e-05


def row_norm(rows, gain):
    widened = rows.astype(jnp.float32)
    return (
        widened
        * lax.rsqrt(jnp.mean(widened * widened, axis=1, keepdims=True) + norm_epsilon)
        * gain
    ).astype(jnp.bfloat16)


def pack_slots(tokens, destination, slot_index, groups, capacity):
    return (
        jnp.zeros((groups, capacity, tokens.shape[1]), jnp.bfloat16)
        .at[destination, slot_index]
        .set(tokens)
    )


def local(
    text_embeds,
    vision_tokens,
    vision_request,
    image_start,
    lengths,
    attn_gain,
    w_query,
    w_key,
    w_value,
    w_out,
    final_gain,
    lm_head,
):
    groups = lax.axis_size("fsdp")
    seq_count = lax.axis_size("seq")
    group_index = lax.axis_index("fsdp")
    seq_index = lax.axis_index("seq")
    seq_len = text_embeds.shape[0]
    width = text_embeds.shape[1]
    columns = w_key.shape[1]
    heads_local = columns // HD
    dpiece = width // groups
    fpiece = width // seq_count
    quarter = groups // seq_count
    capacity = max(2, 2 * vision_tokens.shape[0] // groups)
    last_index = lengths[0] - 1
    destination = vision_request[:, 0]
    onehot = (destination[:, None] == jnp.arange(groups, dtype=jnp.int32)[None, :]).astype(
        jnp.int32
    )
    slot_index = jnp.sum((jnp.cumsum(onehot, axis=0) - onehot) * onehot, axis=1)
    counts = jnp.sum(onehot, axis=0)
    outbox = pack_slots(vision_tokens, destination, slot_index, groups, capacity)
    final_text = lax.dynamic_slice_in_dim(text_embeds, last_index, 1, 0)
    last_row = row_norm(final_text, attn_gain)
    last_pieces = jnp.stack(
        [last_row.reshape(groups, dpiece), final_text.reshape(groups, dpiece)], axis=1
    )
    last_parts = lax.all_to_all(last_pieces, "fsdp", split_axis=0, concat_axis=0, tiled=True)
    received = lax.all_to_all(outbox, "fsdp", split_axis=0, concat_axis=0, tiled=True)
    arrived = lax.all_to_all(counts[:, None], "fsdp", split_axis=0, concat_axis=0, tiled=True)
    query = lax.psum(
        jnp.dot(last_parts[:, 0], w_query, preferred_element_type=jnp.float32), "fsdp"
    ).astype(jnp.bfloat16)
    gain_part = lax.dynamic_slice_in_dim(attn_gain, group_index * dpiece, dpiece, 0)
    probe_part = (
        jnp.einsum(
            "rhc,dhc->rhd",
            query.reshape(groups, heads_local, HD),
            w_key.reshape(dpiece, heads_local, HD),
            preferred_element_type=jnp.float32,
        )
        * gain_part
    ).astype(jnp.bfloat16)
    probe = lax.all_to_all(probe_part, "fsdp", split_axis=0, concat_axis=0, tiled=True)
    probe = probe.transpose(1, 0, 2).reshape(heads_local, width)
    probe = lax.all_to_all(probe, "seq", split_axis=1, concat_axis=0, tiled=True)
    occupied = (
        (jnp.arange(capacity, dtype=jnp.int32)[None, :] < arrived).astype(jnp.int32).reshape(-1)
    )
    ranking = jnp.cumsum(occupied) - occupied
    positions = jnp.where(occupied > 0, image_start[0] + ranking, seq_len)
    text_piece = lax.dynamic_slice_in_dim(text_embeds, seq_index * fpiece, fpiece, 1)
    states = text_piece.at[positions].set(received.reshape(-1, fpiece), mode="drop")
    widened = states.astype(jnp.float32)
    squares = jnp.sum(widened * widened, axis=1)
    partial_scores = jnp.einsum("hd,jd->hj", probe, states, preferred_element_type=jnp.float32)
    summed = lax.psum(jnp.concatenate([partial_scores, squares[None, :]], axis=0), "seq")
    inverse = lax.rsqrt(summed[-1:] / width + norm_epsilon)
    scores = summed[:-1] * inverse / math.sqrt(HD)
    live_keys = jnp.arange(seq_len, dtype=jnp.int32) < lengths[0]
    scores = jnp.where(live_keys[None, :], scores, -jnp.inf)
    peak = jnp.max(scores, axis=1, keepdims=True)
    shifted = jnp.exp(scores - peak)
    weights = shifted / jnp.sum(shifted, axis=1, keepdims=True)
    mixed = jnp.dot(
        (weights * inverse).astype(jnp.bfloat16), states, preferred_element_type=jnp.float32
    )
    mixed_gain = lax.dynamic_slice_in_dim(attn_gain, seq_index * fpiece, fpiece, 0)
    mixed = (mixed * mixed_gain).astype(jnp.bfloat16)
    mixed = lax.all_to_all(mixed, "seq", split_axis=0, concat_axis=1, tiled=True)
    mixed = mixed.reshape(heads_local, groups, dpiece).transpose(1, 0, 2)
    mixed = lax.all_to_all(mixed, "fsdp", split_axis=0, concat_axis=0, tiled=True)
    attended = lax.psum(
        jnp.einsum(
            "rhd,dhc->rhc",
            mixed,
            w_value.reshape(dpiece, heads_local, HD),
            preferred_element_type=jnp.float32,
        ).reshape(groups, columns),
        "fsdp",
    ).astype(jnp.bfloat16)
    out_rows = lax.dynamic_slice_in_dim(w_out, seq_index * columns, columns, 0)
    projected = lax.psum(jnp.dot(attended, out_rows, preferred_element_type=jnp.float32), "seq")
    residual_out = last_parts[:, 1].astype(jnp.float32) + projected
    residual_out = lax.dynamic_slice_in_dim(residual_out, seq_index * quarter, quarter, 0)
    final_part = lax.dynamic_slice_in_dim(final_gain, group_index * dpiece, dpiece, 0)
    scaled_out = (residual_out * final_part[None, :]).astype(jnp.bfloat16)
    square_part = jnp.sum(residual_out * residual_out, axis=1)
    full_scaled = lax.all_gather(scaled_out, "fsdp", axis=1, tiled=True)
    mean_square = lax.psum(square_part, "fsdp") / width
    logits = jnp.dot(full_scaled, lm_head, preferred_element_type=jnp.float32)
    local_max = jnp.max(logits, axis=1) * lax.rsqrt(mean_square + norm_epsilon)
    max_logit = lax.pmax(local_max, "fsdp")
    return (jnp.sqrt(mean_square), max_logit)


def solution(mesh):
    return jax.shard_map(
        local,
        mesh=mesh,
        in_specs=(
            P("fsdp", None),
            P("fsdp", "seq"),
            P("fsdp", None),
            P("fsdp"),
            P("fsdp"),
            P(),
            P("fsdp", "seq"),
            P("fsdp", "seq"),
            P("fsdp", "seq"),
            P(None, "fsdp"),
            P(),
            P(None, "fsdp"),
        ),
        out_specs=(P("seq"), P("seq")),
        check_vma=False,
    )
```

time: 418 us -> 273 us (0.65)
  waiting for transfers between devices: 196 us -> 28.6 us
  blocking collectives: 102 us -> 162 us
  local copies, waits for them, and re-layouts: 51.9 us -> 27.2 us
  between operations: 15.8 us -> 2.94 us
  starting transfers between devices: 17 us -> 25.9 us
  matrix products: 26.5 us -> 17.7 us
    all_gather x4 -> x0, waiting for transfers between devices: 120 us -> none  [the longest x1 68.8 us: local(): lax.all_gather(w_value, 'fsdp', axis=0, tiled=True)]
    psum x0 -> x5, blocking collectives: none -> 109 us  [the longest x1 37.5 us: local(): lax.psum(jnp.dot(last_parts[:, 0], w_query, preferred_element_type=jnp.fl...]
    all_to_all x1, waiting for transfers between devices: 71.7 us -> 14.4 us  [local(): lax.all_to_all(outbox, 'fsdp', split_axis=0, concat_axis=0, tiled=True)]
    all_gather x2 -> x1, blocking collectives: 65.1 us -> 26 us  [local(): full_scaled = lax.all_gather(scaled_out, 'fsdp', axis=1, tiled=True)]
    unnamed x1 -> x0, blocking collectives: 17.1 us -> none
    all_to_all x1 -> x4, starting transfers between devices: 3.43 us -> 19.2 us  [the longest x1 7.28 us: local(): lax.all_to_all(last_pieces, 'fsdp', split_axis=0, concat_axis=0, tiled=True)]
    scatter x1, local copies, waits for them, and re-layouts: 33.9 us -> 19.1 us  [pack_slots(): return jnp.zeros((groups, capacity, tokens.shape[1]), jnp.bfloat16).at[de...]
    all_to_all x1 -> x4, waiting for transfers between devices: 0.01 us -> 14.2 us  [the longest x1 5.92 us: local(): lax.all_to_all(mixed, 'fsdp', split_axis=0, concat_axis=0, tiled=True)]
  transfers between devices with their start and end apart: 7 -> 6, of which waited for: 4 -> 4; matrix products, arithmetic and copies ran while one was open for 15% -> 11% of each run, Pallas kernels for 0% -> 0%
where the time goes in v1:
time: 273 us; the launch traced here: 271 us
  blocking collectives  162 us (59%)
  waiting for transfers between devices  28.6 us (10%)
  local copies, waits for them, and re-layouts  27.2 us (10%)
  starting transfers between devices  25.9 us (9%)
  matrix products  17.7 us (6%)
  other arithmetic  7.24 us (3%)
  between operations  2.94 us (1%)
    psum x1, blocking collectives, local(): lax.psum(jnp.dot(last_parts[:, 0], w_query, preferred_element_type=jnp.fl...  37.5 us
    psum x1, blocking collectives, local(): lax.psum(jnp.einsum('rhd,dhc->rhc', mixed, w_value.reshape(dpiece, heads_...  33.5 us
    all_gather x1, blocking collectives, local(): full_scaled = lax.all_gather(scaled_out, 'fsdp', axis=1, tiled=True)  26 us
    pmax x1, blocking collectives, local(): max_logit = lax.pmax(local_max, 'fsdp')  19.6 us
    scatter x1, local copies, waits for them, and re-layouts, pack_slots(): return jnp.zeros((groups, capacity, tokens.shape[1]), jnp.bfloat16).at[de...  19.1 us
    psum x1, blocking collectives, local(): mean_square = lax.psum(square_part, 'fsdp') / width  17.1 us
    all_to_all x1, waiting for transfers between devices, local(): lax.all_to_all(outbox, 'fsdp', split_axis=0, concat_axis=0, tiled=True)  14.4 us
    dot_general x1, matrix products, local(): logits = jnp.dot(full_scaled, lm_head, preferred_element_type=jnp.float32)  14.3 us
  transfers between devices with their start and end apart: 6, of which 4 were waited for; matrix products, arithmetic and copies ran while one was open for 11% of the time, Pallas kernels for 0%

profile of v1, /device:TPU:0, one launch (start us, length us, event | category | flops | bytes accessed | tf_op | source)
XLA Modules:
  0.0 271.3 jit_solution(3386977346432392454)
XLA Ops:
  1.5 1.5 multiply_reduce_fusion.1
  3.6 0.7 multiply_convert_fusion.1
  5.0 7.3 %all-to-all-start = ((bf16[8,2,512]{2,1,0:T(2,128)(2,1)}), bf16[8,2,512]{2,1,0:T(2,128)(2,1)S(1)}, u32[]{:S(2)}, u32[]{:S(2)}) async-start(bf16[8,2,512]{2,1,0:T(2,128)(2,1)} %pad_maximum_fusion.1), calls=%async_computation | async-start | bytes 32768 | tf_op jit(solution)/shard_map/all_to_all | solution.py:70
  12.3 0.7 fusion.9
  13.2 0.8 select_reduce_fusion
  15.4 0.8 dynamic_slice.22
  16.1 2.7 %all-to-all-done = bf16[8,2,512]{2,1,0:T(2,128)(2,1)S(1)} async-done(((bf16[8,2,512]{2,1,0:T(2,128)(2,1)}), bf16[8,2,512]{2,1,0:T(2,128)(2,1)S(1)}, u32[]{:S(2)}, u32[]{:S(2)}) %all-to-all-start) | async-done | bytes 16416 | tf_op jit(solution)/shard_map/all_to_all | solution.py:70
  18.9 3.3 %all-to-all-start.3 = ((s32[8,1,1]{2,1,0:T(1,128)}), s32[8,1,1]{2,1,0:T(1,128)S(1)}, u32[]{:S(2)}, u32[]{:S(2)}) async-start(s32[8,1,1]{2,1,0:T(1,128)} %copy.31), calls=%async_computation.3 | async-start | bytes 8192 | tf_op jit(solution)/shard_map/all_to_all | solution.py:72
  22.2 1.2 fusion.22
  23.4 37.5 %psum.35 = bf16[8,512]{1,0:T(8,128)(2,1)S(1)} all-reduce(f32[8,512]{1,0:T(8,128)S(1)} %fusion.22), channel_id=1, replica_groups=mesh['fsdp'=8,'seq'=4] {'fsdp'}, use_global_device_ids=true, to_apply=%region_1.2 | all-reduce | flops 4096 | bytes 24576 | tf_op jit(solution)/shard_map/psum | solution.py:73
  61.0 1.3 fusion.2
  62.9 4.0 %all-to-all-start.1 = ((bf16[8,4,512]{2,1,0:T(4,128)(2,1)}), bf16[8,4,512]{2,1,0:T(4,128)(2,1)}, u32[]{:S(2)}, u32[]{:S(2)}) async-start(bf16[8,4,512]{2,1,0:T(4,128)(2,1)} %copy.30), calls=%async_computation.1 | async-start | bytes 65536 | tf_op jit(solution)/shard_map/all_to_all | solution.py:86
  66.8 1.1 constant_dynamic-slice_fusion
  67.9 5.6 %all-to-all-done.1 = bf16[8,4,512]{2,1,0:T(4,128)(2,1)} async-done(((bf16[8,4,512]{2,1,0:T(4,128)(2,1)}), bf16[8,4,512]{2,1,0:T(4,128)(2,1)}, u32[]{:S(2)}, u32[]{:S(2)}) %all-to-all-start.1) | async-done | bytes 32800 | tf_op jit(solution)/shard_map/all_to_all | solution.py:86
  73.5 3.3 %all-to-all-start.2 = ((bf16[4,4,1024]{2,0,1:T(4,128)(2,1)}), bf16[4,4,1024]{2,0,1:T(4,128)(2,1)S(1)}, u32[]{:S(2)}, u32[]{:S(2)}) async-start(bf16[4,4,1024]{2,0,1:T(4,128)(2,1)} %bitcast.9), calls=%async_computation.2 | async-start | bytes 65536 | tf_op jit(solution)/shard_map/all_to_all | solution.py:88
  76.8 0.7 dynamic_slice.24
  78.3 0.9 broadcast_in_dim.25
  79.1 19.1 %scatter_fusion = bf16[8,32,1024]{2,1,0:T(8,128)(2,1)} fusion(bf16[8,32,1024]{2,1,0:T(8,128)(2,1)} %broadcast_in_dim.25, s32[128]{0:T(128)S(1)} %fusion.32, bf16[128,1024]{1,0:T(8,128)(2,1)S(1)} %copy-done.2), kind=kCustom, calls=%fused_computation | custom fusion | bytes 787456 | tf_op jit(solution)/shard_map/scatter | solution.py:27
  98.6 3.5 %all-to-all-start.4 = ((bf16[8,32,1024]{2,1,0:T(8,128)(2,1)}), bf16[8,32,1024]{2,1,0:T(8,128)(2,1)S(1)}, u32[]{:S(2)}, u32[]{:S(2)}) async-start(bf16[8,32,1024]{2,1,0:T(8,128)(2,1)} %scatter_fusion), calls=%async_computation.4 | async-start | bytes 1048576 | tf_op jit(solution)/shard_map/all_to_all | solution.py:71
  103.1 14.4 %all-to-all-done.4 = bf16[8,32,1024]{2,1,0:T(8,128)(2,1)S(1)} async-done(((bf16[8,32,1024]{2,1,0:T(8,128)(2,1)}), bf16[8,32,1024]{2,1,0:T(8,128)(2,1)S(1)}, u32[]{:S(2)}, u32[]{:S(2)}) %all-to-all-start.4) | async-done | bytes 524320 | tf_op jit(solution)/shard_map/all_to_all | solution.py:71
  117.4 1.9 scatter_fusion.1
  119.9 10.7 %psum.36 = f32[17,280]{1,0:T(8,128)S(1)} all-reduce(f32[17,280]{1,0:T(8,128)S(1)} %pad_maximum_fusion), channel_id=1, replica_groups=mesh['fsdp'=8,'seq'=4] {'seq'}, use_global_device_ids=true, to_apply=%region_10.11 | all-reduce | flops 4760 | bytes 38080 | tf_op jit(solution)/shard_map/psum | solution.py:99
  131.2 7.0 %all_to_all.64 = bf16[4,4,1024]{2,1,0:T(4,128)(2,1)} all-to-all(bf16[4,4,1024]{2,1,0:T(4,128)(2,1)S(1)} %all_to_all.53), channel_id=1, replica_groups=mesh['fsdp'=8,'seq'=4] {'seq'}, dimensions={0} | all-to-all | bytes 65536 | tf_op jit(solution)/shard_map/all_to_all | solution.py:112
  138.2 4.7 %all-to-all-start.6 = ((bf16[8,4,512]{2,1,0:T(4,128)(2,1)}), bf16[8,4,512]{2,1,0:T(4,128)(2,1)S(1)}, u32[]{:S(2)}, u32[]{:S(2)}) async-start(bf16[8,4,512]{2,1,0:T(4,128)(2,1)} %bitcast.21), calls=%async_computation.6 | async-start | bytes 65536 | tf_op jit(solution)/shard_map/all_to_all | solution.py:114
  142.8 0.8 dynamic_slice.27
  143.6 5.9 %all-to-all-done.6 = bf16[8,4,512]{2,1,0:T(4,128)(2,1)S(1)} async-done(((bf16[8,4,512]{2,1,0:T(4,128)(2,1)}), bf16[8,4,512]{2,1,0:T(4,128)(2,1)S(1)}, u32[]{:S(2)}, u32[]{:S(2)}) %all-to-all-start.6) | async-done | bytes 32800 | tf_op jit(solution)/shard_map/all_to_all | solution.py:114
  149.7 33.5 %psum.37 = bf16[8,512]{1,0:T(8,128)(2,1)S(1)} all-reduce(f32[8,512]{1,0:T(8,128)S(1)} %convolution_bitcast_fusion), channel_id=1, replica_groups=mesh['fsdp'=8,'seq'=4] {'fsdp'}, use_global_device_ids=true, to_apply=%region_13.14 | all-reduce | flops 4096 | bytes 24576 | tf_op jit(solution)/shard_map/psum | solution.py:115
  183.4 10.1 %psum.38 = f32[8,512]{1,0:T(8,128)S(1)} all-reduce(f32[8,512]{1,0:T(8,128)S(1)} %fusion.7), channel_id=1, replica_groups=mesh['fsdp'=8,'seq'=4] {'seq'}, use_global_device_ids=true, to_apply=%region_14.15 | all-reduce | flops 4096 | bytes 32768 | tf_op jit(solution)/shard_map/psum | solution.py:125
  193.7 26.0 %all_gather.3 = bf16[2,4096]{1,0:T(2,128)(2,1)S(1)} all-gather(bf16[2,512]{1,0:T(2,128)(2,1)S(1)} %get-tuple-element.6), channel_id=1, replica_groups=mesh['fsdp'=8,'seq'=4] {'fsdp'}, dimensions={1}, use_global_device_ids=true | all-gather | bytes 18432 | tf_op jit(solution)/shard_map/all_gather | solution.py:131
  219.6 17.1 %psum.39 = f32[2]{0:T(128)S(1)} all-reduce(f32[2]{0:T(128)S(1)} %get-tuple-element.7), channel_id=1, replica_groups=mesh['fsdp'=8,'seq'=4] {'fsdp'}, use_global_device_ids=true, to_apply=%region_16.17 | all-reduce | flops 2 | bytes 16 | tf_op jit(solution)/shard_map/psum | solution.py:132
  236.8 14.3 %convolution_reduce_fusion = f32[2]{0:T(128)S(1)} fusion(bf16[2,4096]{1,0:T(2,128)(2,1)S(1)} %all_gather.3, bf16[4096,4000]{0,1:T(8,128)(2,1)} %param.23), kind=kOutput, calls=%fused_computation.8 | convolution fusion | flops 65544000 | bytes 32784392 | tf_op jit(solution)/shard_map/dot_general | solution.py:133
  251.6 19.6 %pmax.7 = f32[2]{0:T(128)} all-reduce(f32[2]{0:T(128)S(1)} %get-tuple-element.10), channel_id=1, replica_groups=mesh['fsdp'=8,'seq'=4] {'fsdp'}, use_global_device_ids=true, to_apply=%region_18.19 | all-reduce | flops 2 | bytes 16 | tf_op jit(solution)/shard_map/pmax | solution.py:135
  (45 shorter events, 6.3 us)
Async XLA Ops:
  0.6 182.6 %copy-start = (bf16[2048,512]{1,0:T(8,128)(2,1)S(1)}, bf16[2048,512]{1,0:T(8,128)(2,1)}, u32[]{:S(2)}) copy-start(bf16[2048,512]{1,0:T(8,128)(2,1)} %param.21) | copy-start | bytes 6291460
  0.6 78.5 %copy-start.2 = (bf16[128,1024]{1,0:T(8,128)(2,1)S(1)}, bf16[128,1024]{1,0:T(8,128)(2,1)}, u32[]{:S(2)}) copy-start(bf16[128,1024]{1,0:T(8,128)(2,1)} %param.13) | copy-start | bytes 786436
  5.0 13.9 %all-to-all-start = ((bf16[8,2,512]{2,1,0:T(2,128)(2,1)}), bf16[8,2,512]{2,1,0:T(2,128)(2,1)S(1)}, u32[]{:S(2)}, u32[]{:S(2)}) async-start(bf16[8,2,512]{2,1,0:T(2,128)(2,1)} %pad_maximum_fusion.1), calls=%async_computation | async-start | bytes 32768 | tf_op jit(solution)/shard_map/all_to_all | solution.py:70
  18.9 44.0 %all-to-all-start.3 = ((s32[8,1,1]{2,1,0:T(1,128)}), s32[8,1,1]{2,1,0:T(1,128)S(1)}, u32[]{:S(2)}, u32[]{:S(2)}) async-start(s32[8,1,1]{2,1,0:T(1,128)} %copy.31), calls=%async_computation.3 | async-start | bytes 8192 | tf_op jit(solution)/shard_map/all_to_all | solution.py:72
  62.9 10.7 %all-to-all-start.1 = ((bf16[8,4,512]{2,1,0:T(4,128)(2,1)}), bf16[8,4,512]{2,1,0:T(4,128)(2,1)}, u32[]{:S(2)}, u32[]{:S(2)}) async-start(bf16[8,4,512]{2,1,0:T(4,128)(2,1)} %copy.30), calls=%async_computation.1 | async-start | bytes 65536 | tf_op jit(solution)/shard_map/all_to_all | solution.py:86
  73.5 25.0 %all-to-all-start.2 = ((bf16[4,4,1024]{2,0,1:T(4,128)(2,1)}), bf16[4,4,1024]{2,0,1:T(4,128)(2,1)S(1)}, u32[]{:S(2)}, u32[]{:S(2)}) async-start(bf16[4,4,1024]{2,0,1:T(4,128)(2,1)} %bitcast.9), calls=%async_computation.2 | async-start | bytes 65536 | tf_op jit(solution)/shard_map/all_to_all | solution.py:88
  98.6 18.9 %all-to-all-start.4 = ((bf16[8,32,1024]{2,1,0:T(8,128)(2,1)}), bf16[8,32,1024]{2,1,0:T(8,128)(2,1)S(1)}, u32[]{:S(2)}, u32[]{:S(2)}) async-start(bf16[8,32,1024]{2,1,0:T(8,128)(2,1)} %scatter_fusion), calls=%async_computation.4 | async-start | bytes 1048576 | tf_op jit(solution)/shard_map/all_to_all | solution.py:71
  119.4 30.2 %copy-start.1 = (bf16[512,512]{1,0:T(8,128)(2,1)S(1)}, bf16[512,512]{1,0:T(8,128)(2,1)}, u32[]{:S(2)}) copy-start(bf16[512,512]{1,0:T(8,128)(2,1)} %param.20) | copy-start | bytes 1572868
  138.2 11.3 %all-to-all-start.6 = ((bf16[8,4,512]{2,1,0:T(4,128)(2,1)}), bf16[8,4,512]{2,1,0:T(4,128)(2,1)S(1)}, u32[]{:S(2)}, u32[]{:S(2)}) async-start(bf16[8,4,512]{2,1,0:T(4,128)(2,1)} %bitcast.21), calls=%async_computation.6 | async-start | bytes 65536 | tf_op jit(solution)/shard_map/all_to_all | solution.py:114

commit v2 on v1

--- a/solution.py
+++ b/solution.py
@@ -1,8 +1,11 @@
+import functools
 import math
 
 import jax
 import jax.numpy as jnp
 from jax import lax
+from jax.experimental import pallas as pl
+from jax.experimental.pallas import tpu as pltpu
 from jax.sharding import PartitionSpec as P
 
 HD = 128
@@ -136,9 +139,500 @@
     return (jnp.sqrt(mean_square), max_logit)
 
 
+MESH = pl.DeviceIdType.MESH
+F32 = jnp.float32
+BF16 = jnp.bfloat16
+
+
+def dot(a, b):
+    return jnp.dot(a, b, preferred_element_type=F32)
+
+
+def dot_rows(a, b):
+    return lax.dot_general(a, b, (((1,), (1,)), ((), ())), preferred_element_type=F32)
+
+
+def iota(shape, axis):
+    return lax.broadcasted_iota(jnp.int32, shape, axis)
+
+
+def fused_kernel(
+    groups,
+    seq_count,
+    capacity,
+    request,
+    start,
+    lengths,
+    attn_gain,
+    final_gain,
+    text_hbm,
+    vision_hbm,
+    wq_hbm,
+    wk_hbm,
+    wv_hbm,
+    wo_hbm,
+    lm_hbm,
+    rms_out,
+    max_out,
+    text,
+    vision,
+    wq,
+    wk,
+    wv,
+    wo,
+    lm,
+    states,
+    heads_in,
+    last_send,
+    last_recv,
+    box_send,
+    box_recv,
+    count_send,
+    count_recv,
+    query_send,
+    query_recv,
+    key_send,
+    key_recv,
+    score_recv,
+    mix_send,
+    mix_recv,
+    att_send,
+    att_recv,
+    out_recv,
+    scaled_send,
+    scaled_recv,
+    logit_send,
+    logit_recv,
+    peak_recv,
+    local_sem,
+    send_sem,
+    recv_sem,
+):
+    f = lax.axis_index("fsdp")
+    s = lax.axis_index("seq")
+    devices = groups * seq_count
+    seq_len, width = text.shape
+    rows_per = width // groups
+    piece = width // seq_count
+    owners = groups // seq_count
+    columns = wq.shape[1]
+    local_heads = columns // HD
+    heads = local_heads * seq_count
+    vtok = vision.shape[0]
+    half = rows_per // 2
+
+    barrier = pltpu.get_barrier_semaphore()
+    me = f * seq_count + s
+
+    def greet(k, carry):
+        t = lax.rem(me + k, devices)
+        pl.semaphore_signal(
+            barrier,
+            inc=1,
+            device_id=(lax.div(t, seq_count), lax.rem(t, seq_count)),
+            device_id_type=MESH,
+        )
+        return carry
+
+    lax.fori_loop(1, devices, greet, 0)
+
+    def fetch(index, source, target):
+        copy = pltpu.make_async_copy(source, target, local_sem.at[index])
+        copy.start()
+        return copy
+
+    get_text = fetch(0, text_hbm, text)
+    get_vision = fetch(1, vision_hbm, vision)
+    get_wq = fetch(2, wq_hbm, wq)
+    get_wk = fetch(3, wk_hbm, wk)
+    get_wv = fetch(4, wv_hbm, wv)
+    get_wo = fetch(5, wo_hbm.at[pl.ds(pl.multiple_of(s * columns, columns), columns)], wo)
+    get_lm = fetch(6, lm_hbm.at[pl.ds(pl.multiple_of(s * piece, piece), piece)], lm)
+
+    sent = []
+
+    def copy_of(phase, slot, from_slot, source, target, to_f, to_s):
+        return pltpu.make_async_remote_copy(
+            src_ref=source,
+            dst_ref=target,
+            send_sem=send_sem.at[phase, slot],
+            recv_sem=recv_sem.at[phase, from_slot],
+            device_id=(to_f, to_s),
+            device_id_type=MESH,
+        )
+
+    def push(*what):
+        copy = copy_of(*what)
+        copy.start()
+        sent.append(copy)
+
+    def arrive(phase, slot, target):
+        copy_of(phase, 0, slot, target, target, f, s).wait_recv()
+
+    def across_groups(phase, source, target):
+        for k in range(1, groups):
+            t = lax.rem(f + k, groups)
+            push(phase, k, f, source(t), target(f), t, s)
+
+    def from_groups(phase, target):
+        for k in range(1, groups):
+            o = lax.rem(f + groups - k, groups)
+            arrive(phase, o, target(o))
+
+    def across_seq(phase, source, target):
+        for k in range(1, seq_count):
+            t = lax.rem(s + k, seq_count)
+            push(phase, k, s, source(t), target(s), f, t)
+
+    def from_seq(phase, target):
+        for k in range(1, seq_count):
+            o = lax.rem(s + seq_count - k, seq_count)
+            arrive(phase, o, target(o))
+
+    length = lengths[0]
+    tail = (seq_len - 8) // 16 * 16
+    get_text.wait()
+    tail_rows = text[tail:, :].astype(F32)
+    here = iota((seq_len - tail, 1), 0) == length - 1 - tail
+    last = jnp.sum(jnp.where(here, tail_rows, 0.0), axis=0, keepdims=True)
+    scale = lax.rsqrt(jnp.mean(last * last, axis=1, keepdims=True) + norm_epsilon)
+    normed = (last * scale * attn_gain[...]).astype(BF16).astype(F32)
+    for g in range(groups):
+        span = slice(g * rows_per, (g + 1) * rows_per)
+        last_send[g, 0:1, :] = normed[:, span]
+        last_send[g, 1:2, :] = last[:, span]
+    last_recv[f] = last_send[f]
+    pl.semaphore_wait(barrier, devices - 1)
+    across_groups(0, lambda t: last_send.at[t], lambda me_f: last_recv.at[me_f])
+
+    named = request[...]
+    member = jnp.where(iota((groups, vtok), 0) == named, 1.0, 0.0)
+    earlier = jnp.where(iota((vtok, vtok), 0) < iota((vtok, vtok), 1), 1.0, 0.0)
+    before = dot(member.astype(BF16), earlier.astype(BF16))
+    rank = jnp.sum(before * member, axis=0, keepdims=True)
+    counts = jnp.broadcast_to(jnp.sum(member, axis=1, keepdims=True), (groups, 128))
+    for g in range(groups):
+        count_send[g] = counts[g : g + 1, :]
+    count_recv[f] = count_send[f]
+    across_groups(1, lambda t: count_send.at[t], lambda me_f: count_recv.at[me_f])
+    slot = named.astype(F32) * capacity + rank
+    slots = groups * capacity
+    pick = jnp.where(iota((slots, vtok), 0).astype(F32) == slot, 1.0, 0.0).astype(BF16)
+    get_vision.wait()
+    box_send[...] = dot(pick, vision[...]).astype(BF16).reshape(groups, capacity, piece)
+    box_recv[f] = box_send[f]
+    across_groups(2, lambda t: box_send.at[t], lambda me_f: box_recv.at[me_f])
+
+    from_groups(0, lambda o: last_recv.at[o])
+    get_wq.wait()
+    query_part = dot(last_recv[:, 0, :].astype(BF16), wq[...])
+    query_send[...] = query_part
+    query_recv[f] = query_part
+    across_groups(3, lambda t: query_send, lambda me_f: query_recv.at[me_f])
+    get_wk.wait()
+    from_groups(3, lambda o: query_recv.at[o])
+    query = jnp.sum(query_recv[...], axis=0).astype(BF16)
+
+    gain_rows = attn_gain[:, pl.ds(pl.multiple_of(f * rows_per, rows_per), rows_per)]
+    for h in range(local_heads):
+        span = slice(h * HD, (h + 1) * HD)
+        key_send[:, h, :] = dot_rows(query[:, span], wk[:, span]) * gain_rows
+    home = lax.div(f, owners)
+    inner = lax.rem(f, owners)
+    at_home = home == s
+    own_key = copy_of(4, 0, inner * seq_count + s, key_send.at[f], key_recv.at[inner, s], f, home)
+
+    @pl.when(at_home)
+    def _():
+        key_recv[inner, s] = key_send[f]
+
+    @pl.when(jnp.logical_not(at_home))
+    def _():
+        own_key.start()
+
+    for k in range(1, groups):
+        t = lax.rem(f + k, groups)
+        push(4, k, inner * seq_count + s, key_send.at[t], key_recv.at[inner, s], t, home)
+
+    from_groups(1, lambda o: count_recv.at[o])
+    tally = count_recv[:, 0, :]
+    tallies = jnp.concatenate([tally] * (slots // 128), axis=1)
+    source_of = iota((groups, slots), 0)
+    owner = lax.div(iota((groups, slots), 1), capacity)
+    arrived = jnp.sum(jnp.where(source_of == owner, tallies, 0.0), axis=0, keepdims=True)
+    offset = jnp.sum(jnp.where(source_of < owner, tallies, 0.0), axis=0, keepdims=True)
+    within = lax.rem(iota((1, slots), 1), capacity).astype(F32)
+    first = start[0].astype(F32)
+    position = jnp.where(within < arrived, first + offset + within, -1.0)
+    place = jnp.where(iota((seq_len, slots), 0).astype(F32) == position, 1.0, 0.0).astype(BF16)
+    total = jnp.sum(tally[:, :1], axis=0, keepdims=True)
+    row = iota((seq_len, 1), 0).astype(F32)
+    taken = jnp.logical_and(row >= first, row < first + total)
+    from_groups(2, lambda o: box_recv.at[o])
+    step = min(256, piece)
+    ones = jnp.ones((8, step), BF16)
+    squares = jnp.zeros((8, seq_len), F32)
+    for c in range(piece // step):
+        span = slice(c * step, (c + 1) * step)
+        placed = dot(place, box_recv[:, :, span].reshape(slots, step))
+        at = pl.multiple_of(s * piece + c * step, step)
+        value = jnp.where(taken, placed, text[:, pl.ds(at, step)].astype(F32))
+        states[:, span] = value.astype(BF16)
+        square = value * value
+        high = square.astype(BF16)
+        low = (square - high.astype(F32)).astype(BF16)
+        squares = squares + dot_rows(ones, high) + dot_rows(ones, low)
+
+    for b in range(owners):
+        for k in range(seq_count):
+            o = lax.rem(s + k, seq_count)
+            if k:
+                arrive(4, b * seq_count + o, key_recv.at[b, o])
+            else:
+
+                @pl.when(jnp.logical_not(f == s * owners + b))
+                def _(o=o, b=b):
+                    arrive(4, b * seq_count + o, key_recv.at[b, o])
+
+    for o in range(seq_count):
+        for b in range(owners):
+            heads_in[
+                o * local_heads : (o + 1) * local_heads, b * rows_per : (b + 1) * rows_per
+            ] = key_recv[b, o]
+    part = dot_rows(heads_in[...].astype(BF16), states[...])
+    score_recv[s, :heads] = part
+    score_recv[s, heads:] = squares
+    across_seq(5, lambda t: score_recv.at[s], lambda me_s: score_recv.at[me_s])
+    from_seq(5, lambda o: score_recv.at[o])
+    summed = jnp.sum(score_recv[...], axis=0)
+    inverse = lax.rsqrt(summed[heads : heads + 1] / width + norm_epsilon)
+    live = iota((1, seq_len), 1) < length
+    scores = jnp.where(live, summed[:heads] * inverse / math.sqrt(HD), -jnp.inf)
+    shifted = jnp.exp(scores - jnp.max(scores, axis=1, keepdims=True))
+    weights = shifted / jnp.sum(shifted, axis=1, keepdims=True)
+    mixed = dot((weights * inverse).astype(BF16), states[...])
+    mixed = mixed * attn_gain[:, pl.ds(pl.multiple_of(s * piece, piece), piece)]
+
+    for o in range(seq_count):
+        for b in range(owners):
+            mix_send[b, o] = mixed[
+                o * local_heads : (o + 1) * local_heads, b * rows_per : (b + 1) * rows_per
+            ]
+    own_mix = []
+    for b in range(owners):
+        t = s * owners + b
+        copy = copy_of(6, b * seq_count, f, mix_send.at[b, s], mix_recv.at[f], t, s)
+        own_mix.append((t, copy))
+
+        @pl.when(f == t)
+        def _(b=b):
+            mix_recv[f] = mix_send[b, s]
+
+        @pl.when(jnp.logical_not(f == t))
+        def _(copy=copy):
+            copy.start()
+
+        for k in range(1, seq_count):
+            o = lax.rem(s + k, seq_count)
+            push(6, b * seq_count + k, f, mix_send.at[b, o], mix_recv.at[f], t, o)
+    get_wv.wait()
+    from_groups(6, lambda o: mix_recv.at[o])
+
+    @pl.when(jnp.logical_not(at_home))
+    def _():
+        arrive(6, f, mix_recv.at[f])
+
+    for h in range(local_heads):
+        span = slice(h * HD, (h + 1) * HD)
+        att_send[:, span] = dot(mix_recv[:, h, :].astype(BF16), wv[:, span])
+    att_recv[f] = att_send[...]
+    across_groups(7, lambda t: att_send, lambda me_f: att_recv.at[me_f])
+    get_wo.wait()
+    from_groups(7, lambda o: att_recv.at[o])
+    attended = jnp.sum(att_recv[...], axis=0).astype(BF16)
+
+    out_recv[s] = dot(attended, wo[...])
+    across_seq(8, lambda t: out_recv.at[s], lambda me_s: out_recv.at[me_s])
+    from_seq(8, lambda o: out_recv.at[o])
+    residual = last_recv[:, 1, :] + jnp.sum(out_recv[...], axis=0)
+    square_part = jnp.sum(residual * residual, axis=1, keepdims=True)
+    final_rows = final_gain[:, pl.ds(pl.multiple_of(f * rows_per, rows_per), rows_per)]
+    scaled = residual * final_rows
+    scaled_send[...] = jnp.concatenate([scaled[:, :half], scaled[:, half:]], axis=0).astype(BF16)
+
+    scaled_out = [
+        copy_of(
+            9,
+            k,
+            inner,
+            scaled_send,
+            scaled_recv.at[inner],
+            lax.rem(f + k, groups),
+            s,
+        )
+        for k in range(1, groups)
+    ]
+
+    @pl.when(at_home)
+    def _():
+        scaled_recv[inner] = scaled_send[...]
+        for copy in scaled_out:
+            copy.start()
+
+    get_lm.wait()
+    for b in range(owners):
+
+        @pl.when(jnp.logical_not(f == s * owners + b))
+        def _(b=b):
+            arrive(9, b, scaled_recv.at[b])
+
+    logits = jnp.zeros((groups, lm.shape[1]), F32)
+    for b in range(owners):
+        for c in range(2):
+            at = b * rows_per + c * half
+            logits = logits + dot(
+                scaled_recv[b, c * groups : (c + 1) * groups, :], lm[at : at + half, :]
+            )
+    for o in range(seq_count):
+        logit_send[o] = logits[o * owners : (o + 1) * owners]
+    logit_recv[s] = logit_send[s]
+    across_seq(10, lambda t: logit_send.at[t], lambda me_s: logit_recv.at[me_s])
+    from_seq(10, lambda o: logit_recv.at[o])
+    top = jnp.max(jnp.sum(logit_recv[...], axis=0), axis=1, keepdims=True)
+    mine = iota((owners, groups), 1) - s * owners == iota((owners, groups), 0)
+    squares_row = jnp.sum(
+        jnp.where(iota((groups, groups), 0) == iota((groups, groups), 1), square_part, 0.0),
+        axis=0,
+        keepdims=True,
+    )
+    square_mine = jnp.sum(jnp.where(mine, squares_row, 0.0), axis=1, keepdims=True)
+    lane = iota((owners, 128), 1)
+    peak_recv[f] = jnp.where(lane < 64, top, square_mine)
+    across_groups(11, lambda t: peak_recv.at[f], lambda me_f: peak_recv.at[me_f])
+    from_groups(11, lambda o: peak_recv.at[o])
+    everyone = peak_recv[...]
+    best = jnp.max(everyone, axis=0)[:, :1]
+    mean_square = jnp.sum(everyone, axis=0)[:, 64:65] / width
+    rms_out[...] = jnp.broadcast_to(jnp.sqrt(mean_square), (owners, 128))
+    max_out[...] = jnp.broadcast_to(best * lax.rsqrt(mean_square + norm_epsilon), (owners, 128))
+
+    for copy in sent:
+        copy.wait_send()
+
+    @pl.when(jnp.logical_not(at_home))
+    def _():
+        own_key.wait_send()
+
+    for t, copy in own_mix:
+
+        @pl.when(jnp.logical_not(f == t))
+        def _(copy=copy):
+            copy.wait_send()
+
+    @pl.when(at_home)
+    def _():
+        for copy in scaled_out:
+            copy.wait_send()
+
+
+def fused(
+    text_embeds,
+    vision_tokens,
+    vision_request,
+    image_start,
+    lengths,
+    attn_gain,
+    w_query,
+    w_key,
+    w_value,
+    w_out,
+    final_gain,
+    lm_head,
+):
+    groups = lax.axis_size("fsdp")
+    seq_count = lax.axis_size("seq")
+    seq_len, width = text_embeds.shape
+    vtok, piece = vision_tokens.shape
+    rows_per, columns = w_query.shape
+    vocab = lm_head.shape[1]
+    owners = groups // seq_count
+    local_heads = columns // HD
+    heads = local_heads * seq_count
+    capacity = 2 * vtok // groups
+    vmem = pl.BlockSpec(memory_space=pltpu.VMEM)
+    smem = pl.BlockSpec(memory_space=pltpu.SMEM)
+    any_space = pl.BlockSpec(memory_space=pl.ANY)
+    phases = 12
+    links = max(groups, owners * seq_count)
+    rms, best = pl.pallas_call(
+        functools.partial(fused_kernel, groups, seq_count, capacity),
+        out_shape=[jax.ShapeDtypeStruct((owners, 128), F32)] * 2,
+        in_specs=[vmem, smem, smem, vmem, vmem] + [any_space] * 7,
+        out_specs=[vmem, vmem],
+        scratch_shapes=[
+            pltpu.VMEM((seq_len, width), BF16),
+            pltpu.VMEM((vtok, piece), BF16),
+            pltpu.VMEM((rows_per, columns), BF16),
+            pltpu.VMEM((rows_per, columns), BF16),
+            pltpu.VMEM((rows_per, columns), BF16),
+            pltpu.VMEM((columns, rows_per), BF16),
+            pltpu.VMEM((piece, vocab), BF16),
+            pltpu.VMEM((seq_len, piece), BF16),
+            pltpu.VMEM((heads, piece), F32),
+            pltpu.VMEM((groups, 2, rows_per), F32),
+            pltpu.VMEM((groups, 2, rows_per), F32),
+            pltpu.VMEM((groups, capacity, piece), BF16),
+            pltpu.VMEM((groups, capacity, piece), BF16),
+            pltpu.VMEM((groups, 1, 128), F32),
+            pltpu.VMEM((groups, 1, 128), F32),
+            pltpu.VMEM((groups, columns), F32),
+            pltpu.VMEM((groups, groups, columns), F32),
+            pltpu.VMEM((groups, local_heads, rows_per), F32),
+            pltpu.VMEM((owners, seq_count, local_heads, rows_per), F32),
+            pltpu.VMEM((seq_count, heads + 8, seq_len), F32),
+            pltpu.VMEM((owners, seq_count, local_heads, rows_per), F32),
+            pltpu.VMEM((groups, local_heads, rows_per), F32),
+            pltpu.VMEM((groups, columns), F32),
+            pltpu.VMEM((groups, groups, columns), F32),
+            pltpu.VMEM((seq_count, groups, rows_per), F32),
+            pltpu.VMEM((2 * groups, rows_per // 2), BF16),
+            pltpu.VMEM((owners, 2 * groups, rows_per // 2), BF16),
+            pltpu.VMEM((seq_count, owners, vocab), F32),
+            pltpu.VMEM((seq_count, owners, vocab), F32),
+            pltpu.VMEM((groups, owners, 128), F32),
+            pltpu.SemaphoreType.DMA((7,)),
+            pltpu.SemaphoreType.DMA((phases, links)),
+            pltpu.SemaphoreType.DMA((phases, links)),
+        ],
+        compiler_params=pltpu.CompilerParams(
+            collective_id=0, has_side_effects=True, vmem_limit_bytes=48 * 2**20
+        ),
+        name="fused",
+    )(
+        vision_request.reshape(1, vtok),
+        image_start,
+        lengths,
+        attn_gain.reshape(1, width),
+        final_gain.reshape(1, width),
+        text_embeds,
+        vision_tokens,
+        w_query,
+        w_key,
+        w_value,
+        w_out,
+        lm_head,
+    )
+    return rms[:, 0], best[:, 0]
+
+
+def fits(mesh):
+    groups, seq_count = mesh.shape["fsdp"], mesh.shape["seq"]
+    return groups == 8 and groups % seq_count == 0
+
+
 def solution(mesh):
     return jax.shard_map(
-        local,
+        fused if fits(mesh) else local,
         mesh=mesh,
         in_specs=(
             P("fsdp", None),

time: 273 us -> 105 us (0.38)
  blocking collectives: 162 us -> 0 us
  Pallas kernels: 0 us -> 58.2 us
  waiting for transfers between devices: 28.6 us -> 0 us
  starting transfers between devices: 25.9 us -> 0 us
  matrix products: 17.7 us -> 0 us
  local copies, waits for them, and re-layouts: 27.2 us -> 43.5 us
  other arithmetic: 7.24 us -> 0 us
    psum x5 -> x0, blocking collectives: 109 us -> none  [the longest x1 37.5 us: local(): lax.psum(jnp.dot(last_parts[:, 0], w_query, preferred_element_type=jnp.fl...]
    pallas_call x0 -> x1, Pallas kernels: none -> 58.2 us  [fused(): pl.pallas_call(functools.partial(fused_kernel, groups, seq_count, capacit...]
    unnamed x7 -> x17, local copies, waits for them, and re-layouts: 0.02 us -> 42.8 us
    all_to_all x6 -> x0, waiting for transfers between devices: 28.6 us -> none  [the longest x1 14.4 us: local(): lax.all_to_all(outbox, 'fsdp', split_axis=0, concat_axis=0, tiled=True)]
    all_gather x1 -> x0, blocking collectives: 26 us -> none  [local(): full_scaled = lax.all_gather(scaled_out, 'fsdp', axis=1, tiled=True)]
    all_to_all x6 -> x0, starting transfers between devices: 25.9 us -> none  [the longest x1 7.28 us: local(): lax.all_to_all(last_pieces, 'fsdp', split_axis=0, concat_axis=0, tiled=True)]
    scatter x2 -> x0, local copies, waits for them, and re-layouts: 21.1 us -> none  [the longest x1 19.1 us: pack_slots(): return jnp.zeros((groups, capacity, tokens.shape[1]), jnp.bfloat16).at[de...]
    pmax x1 -> x0, blocking collectives: 19.6 us -> none  [local(): max_logit = lax.pmax(local_max, 'fsdp')]
  transfers between devices with their start and end apart: 6 -> 0, of which waited for: 4 -> 0; matrix products, arithmetic and copies ran while one was open for 11% -> 0% of each run, Pallas kernels for 0% -> 0%
where the time goes in v2:
time: 105 us; the launch traced here: 104 us
  Pallas kernels  58.2 us (55%)
  local copies, waits for them, and re-layouts  43.5 us (41%)
  between operations  2.03 us (2%)
    pallas_call x1, Pallas kernels, fused(): pl.pallas_call(functools.partial(fused_kernel, groups, seq_count, capacit...  58.2 us
    unnamed x17, local copies, waits for them, and re-layouts  42.8 us

profile of v2, /device:TPU:0, one launch (start us, length us, event | category | flops | bytes accessed | tf_op | source)
XLA Modules:
  0.0 103.7 jit_solution(14274288210082295617)
XLA Ops:
  1.9 0.0 copy-start
  1.9 0.0 copy-start.1
  1.9 0.0 copy-start.2
  2.0 0.0 copy-start.4
  2.0 0.0 copy-start.5
  2.0 0.0 copy-start.6
  2.0 0.0 copy-start.7
  2.0 41.8 %copy.15.lm_hbm = bf16[4096,4000]{1,0:T(8,128)(2,1)} copy(bf16[4096,4000]{0,1:T(8,128)(2,1)} %param.23) | data formatting | bytes 65536000 | tf_op args[11]
  43.7 0.0 copy-done
  43.7 0.0 copy-done.1
  43.8 0.0 copy-done.2
  43.8 0.0 copy-done.4
  43.8 0.0 copy-done.5
  43.8 0.0 copy-done.6
  43.8 0.0 copy-done.7
  43.8 0.0 copy-start.3
  43.8 1.0 copy-done.3
  44.8 58.2 %fused.1 = (f32[2,128]{1,0:T(2,128)S(1)}, f32[2,128]{1,0:T(2,128)S(1)}) custom-call(s32[1,128]{1,0:T(1,128)S(1)} %bitcast.5, s32[1]{0:T(128)S(6)} %copy.16.start, s32[1]{0:T(128)S(6)} %copy.17.lengths, f32[1,4096]{1,0:T(1,128)S(1)} %bitcast.3, f32[1,4096]{1,0:T(1,128)S(1)} %bitcast.4, bf16[280,4096]{1,0:T(8,128)(2,1)} %text_hbm.1, ...), custom_call_target="tpu_custom_call" | custom-call | tf_op jit(solution)/shard_map/fused/pallas_call | solution.py:567
  103.0 0.7 slice_reduce_fusion
Async XLA Ops:
  1.9 41.8 %copy-start = (bf16[2048,512]{1,0:T(8,128)(2,1)S(1)}, bf16[2048,512]{1,0:T(8,128)(2,1)}, u32[]{:S(2)}) copy-start(bf16[2048,512]{1,0:T(8,128)(2,1)} %wo_hbm.1) | copy-start | bytes 6291460
  1.9 41.8 %copy-start.1 = (bf16[512,512]{1,0:T(8,128)(2,1)S(1)}, bf16[512,512]{1,0:T(8,128)(2,1)}, u32[]{:S(2)}) copy-start(bf16[512,512]{1,0:T(8,128)(2,1)} %wq_hbm.1) | copy-start | bytes 1572868
  1.9 41.8 %copy-start.2 = (bf16[512,512]{1,0:T(8,128)(2,1)S(1)}, bf16[512,512]{1,0:T(8,128)(2,1)}, u32[]{:S(2)}) copy-start(bf16[512,512]{1,0:T(8,128)(2,1)} %wk_hbm.1) | copy-start | bytes 1572868
  2.0 41.8 %copy-start.4 = (bf16[128,1024]{1,0:T(8,128)(2,1)S(1)}, bf16[128,1024]{1,0:T(8,128)(2,1)}, u32[]{:S(2)}) copy-start(bf16[128,1024]{1,0:T(8,128)(2,1)} %vision_hbm.1) | copy-start | bytes 786436
  2.0 41.8 %copy-start.5 = (f32[4096]{0:T(1024)S(1)}, f32[4096]{0:T(1024)}, u32[]{:S(2)}) copy-start(f32[4096]{0:T(1024)} %param.17) | copy-start | bytes 49156
  2.0 41.8 %copy-start.6 = (f32[4096]{0:T(1024)S(1)}, f32[4096]{0:T(1024)}, u32[]{:S(2)}) copy-start(f32[4096]{0:T(1024)} %param.22) | copy-start | bytes 49156
  2.0 41.8 %copy-start.7 = (s32[128,1]{0,1:T(1,128)S(1)}, s32[128,1]{0,1:T(1,128)}, u32[]{:S(2)}) copy-start(s32[128,1]{0,1:T(1,128)} %param.14) | copy-start | bytes 1540
  43.8 1.0 %copy-start.3 = (bf16[512,512]{1,0:T(8,128)(2,1)S(1)}, bf16[512,512]{1,0:T(8,128)(2,1)}, u32[]{:S(2)}) copy-start(bf16[512,512]{1,0:T(8,128)(2,1)} %wv_hbm.1) | copy-start | bytes 1572868

commit v3 on v2

--- a/solution.py
+++ b/solution.py
@@ -154,6 +154,16 @@
 
 def iota(shape, axis):
     return lax.broadcasted_iota(jnp.int32, shape, axis)
+
+
+def folded(rows):
+    half = rows.shape[1] // 2
+    return jnp.concatenate([rows[:, :half], rows[:, half:]], axis=0).astype(BF16)
+
+
+def unfolded(rows):
+    half = rows.shape[0] // 2
+    return jnp.concatenate([rows[:half], rows[half:]], axis=1)
 
 
 def fused_kernel(
@@ -194,6 +204,7 @@
     key_send,
     key_recv,
     score_recv,
+    square_recv,
     mix_send,
     mix_recv,
     att_send,
@@ -201,8 +212,7 @@
     out_recv,
     scaled_send,
     scaled_recv,
-    logit_send,
-    logit_recv,
+    peak_send,
     peak_recv,
     local_sem,
     send_sem,
@@ -247,7 +257,26 @@
     get_wk = fetch(3, wk_hbm, wk)
     get_wv = fetch(4, wv_hbm, wv)
     get_wo = fetch(5, wo_hbm.at[pl.ds(pl.multiple_of(s * columns, columns), columns)], wo)
-    get_lm = fetch(6, lm_hbm.at[pl.ds(pl.multiple_of(s * piece, piece), piece)], lm)
+    words = lm.shape[0]
+    vocab = lm_hbm.shape[0]
+    final_seq = s == seq_count - 1
+    final_words = vocab - (seq_count - 1) * words
+    get_lm = pltpu.make_async_copy(
+        lm_hbm.at[pl.ds(pl.multiple_of(s * words, words), words)], lm, local_sem.at[6]
+    )
+    get_lm_final = pltpu.make_async_copy(
+        lm_hbm.at[vocab - final_words :], lm.at[:final_words], local_sem.at[6]
+    )
+
+    @pl.when(jnp.logical_not(final_seq))
+    def _():
+        get_lm.start()
+
+    @pl.when(final_seq)
+    def _():
+        get_lm_final.start()
+        if final_words < words:
+            lm[final_words:, :] = jnp.zeros((words - final_words, width), BF16)
 
     sent = []
 
@@ -326,12 +355,12 @@
     from_groups(0, lambda o: last_recv.at[o])
     get_wq.wait()
     query_part = dot(last_recv[:, 0, :].astype(BF16), wq[...])
-    query_send[...] = query_part
-    query_recv[f] = query_part
+    query_send[...] = folded(query_part)
+    query_recv[f] = query_send[...]
     across_groups(3, lambda t: query_send, lambda me_f: query_recv.at[me_f])
     get_wk.wait()
     from_groups(3, lambda o: query_recv.at[o])
-    query = jnp.sum(query_recv[...], axis=0).astype(BF16)
+    query = unfolded(jnp.sum(query_recv[...].astype(F32), axis=0)).astype(BF16)
 
     gain_rows = attn_gain[:, pl.ds(pl.multiple_of(f * rows_per, rows_per), rows_per)]
     for h in range(local_heads):
@@ -383,6 +412,8 @@
         low = (square - high.astype(F32)).astype(BF16)
         squares = squares + dot_rows(ones, high) + dot_rows(ones, low)
 
+    square_recv[s] = squares
+    across_seq(11, lambda t: square_recv.at[s], lambda me_s: square_recv.at[me_s])
     for b in range(owners):
         for k in range(seq_count):
             o = lax.rem(s + k, seq_count)
@@ -400,14 +431,15 @@
                 o * local_heads : (o + 1) * local_heads, b * rows_per : (b + 1) * rows_per
             ] = key_recv[b, o]
     part = dot_rows(heads_in[...].astype(BF16), states[...])
-    score_recv[s, :heads] = part
-    score_recv[s, heads:] = squares
+    score_recv[s] = part
     across_seq(5, lambda t: score_recv.at[s], lambda me_s: score_recv.at[me_s])
     from_seq(5, lambda o: score_recv.at[o])
+    from_seq(11, lambda o: square_recv.at[o])
+    square_sums = jnp.sum(square_recv[...], axis=0)
+    inverse = lax.rsqrt(square_sums[:1] / width + norm_epsilon)
     summed = jnp.sum(score_recv[...], axis=0)
-    inverse = lax.rsqrt(summed[heads : heads + 1] / width + norm_epsilon)
     live = iota((1, seq_len), 1) < length
-    scores = jnp.where(live, summed[:heads] * inverse / math.sqrt(HD), -jnp.inf)
+    scores = jnp.where(live, summed * inverse / math.sqrt(HD), -jnp.inf)
     shifted = jnp.exp(scores - jnp.max(scores, axis=1, keepdims=True))
     weights = shifted / jnp.sum(shifted, axis=1, keepdims=True)
     mixed = dot((weights * inverse).astype(BF16), states[...])
@@ -442,14 +474,16 @@
     def _():
         arrive(6, f, mix_recv.at[f])
 
-    for h in range(local_heads):
-        span = slice(h * HD, (h + 1) * HD)
-        att_send[:, span] = dot(mix_recv[:, h, :].astype(BF16), wv[:, span])
+    att_part = [
+        dot(mix_recv[:, h, :].astype(BF16), wv[:, h * HD : (h + 1) * HD])
+        for h in range(local_heads)
+    ]
+    att_send[...] = folded(jnp.concatenate(att_part, axis=1))
     att_recv[f] = att_send[...]
     across_groups(7, lambda t: att_send, lambda me_f: att_recv.at[me_f])
     get_wo.wait()
     from_groups(7, lambda o: att_recv.at[o])
-    attended = jnp.sum(att_recv[...], axis=0).astype(BF16)
+    attended = unfolded(jnp.sum(att_recv[...].astype(F32), axis=0)).astype(BF16)
 
     out_recv[s] = dot(attended, wo[...])
     across_seq(8, lambda t: out_recv.at[s], lambda me_s: out_recv.at[me_s])
@@ -458,61 +492,45 @@
     square_part = jnp.sum(residual * residual, axis=1, keepdims=True)
     final_rows = final_gain[:, pl.ds(pl.multiple_of(f * rows_per, rows_per), rows_per)]
     scaled = residual * final_rows
-    scaled_send[...] = jnp.concatenate([scaled[:, :half], scaled[:, half:]], axis=0).astype(BF16)
-
-    scaled_out = [
-        copy_of(
-            9,
-            k,
-            inner,
-            scaled_send,
-            scaled_recv.at[inner],
-            lax.rem(f + k, groups),
-            s,
-        )
-        for k in range(1, groups)
-    ]
-
-    @pl.when(at_home)
-    def _():
-        scaled_recv[inner] = scaled_send[...]
-        for copy in scaled_out:
-            copy.start()
-
-    get_lm.wait()
-    for b in range(owners):
-
-        @pl.when(jnp.logical_not(f == s * owners + b))
-        def _(b=b):
-            arrive(9, b, scaled_recv.at[b])
-
-    logits = jnp.zeros((groups, lm.shape[1]), F32)
-    for b in range(owners):
+    scaled_send[...] = folded(scaled)
+
+    scaled_recv[f] = scaled_send[...]
+    across_groups(9, lambda t: scaled_send, lambda me_f: scaled_recv.at[me_f])
+
+    @pl.when(jnp.logical_not(final_seq))
+    def _():
+        get_lm.wait()
+
+    @pl.when(final_seq)
+    def _():
+        get_lm_final.wait()
+
+    logits = jnp.zeros((groups, words), F32)
+    for k in range(groups):
+        o = lax.rem(f + groups - k, groups)
+        if k:
+            arrive(9, o, scaled_recv.at[o])
         for c in range(2):
-            at = b * rows_per + c * half
-            logits = logits + dot(
-                scaled_recv[b, c * groups : (c + 1) * groups, :], lm[at : at + half, :]
+            at = pl.multiple_of(o * rows_per + c * half, half)
+            logits = logits + dot_rows(
+                scaled_recv[o, c * groups : (c + 1) * groups, :], lm[:, pl.ds(at, half)]
             )
+    word = iota((1, words), 1) + s * words
+    top = jnp.max(jnp.where(word < vocab, logits, -jnp.inf), axis=1, keepdims=True)
+    peaks = jnp.where(iota((groups, 128), 1) < 64, top, square_part)
     for o in range(seq_count):
-        logit_send[o] = logits[o * owners : (o + 1) * owners]
-    logit_recv[s] = logit_send[s]
-    across_seq(10, lambda t: logit_send.at[t], lambda me_s: logit_recv.at[me_s])
-    from_seq(10, lambda o: logit_recv.at[o])
-    top = jnp.max(jnp.sum(logit_recv[...], axis=0), axis=1, keepdims=True)
-    mine = iota((owners, groups), 1) - s * owners == iota((owners, groups), 0)
-    squares_row = jnp.sum(
-        jnp.where(iota((groups, groups), 0) == iota((groups, groups), 1), square_part, 0.0),
-        axis=0,
-        keepdims=True,
-    )
-    square_mine = jnp.sum(jnp.where(mine, squares_row, 0.0), axis=1, keepdims=True)
-    lane = iota((owners, 128), 1)
-    peak_recv[f] = jnp.where(lane < 64, top, square_mine)
-    across_groups(11, lambda t: peak_recv.at[f], lambda me_f: peak_recv.at[me_f])
-    from_groups(11, lambda o: peak_recv.at[o])
+        peak_send[o] = peaks[o * owners : (o + 1) * owners]
+    peak_recv[me] = peak_send[s]
+    for k in range(1, devices):
+        t = lax.rem(me + k, devices)
+        t_f, t_s = lax.div(t, seq_count), lax.rem(t, seq_count)
+        push(10, k, me, peak_send.at[t_s], peak_recv.at[me], t_f, t_s)
+    for k in range(1, devices):
+        o = lax.rem(me + devices - k, devices)
+        arrive(10, o, peak_recv.at[o])
     everyone = peak_recv[...]
     best = jnp.max(everyone, axis=0)[:, :1]
-    mean_square = jnp.sum(everyone, axis=0)[:, 64:65] / width
+    mean_square = jnp.sum(everyone, axis=0)[:, 64:65] / (width * seq_count)
     rms_out[...] = jnp.broadcast_to(jnp.sqrt(mean_square), (owners, 128))
     max_out[...] = jnp.broadcast_to(best * lax.rsqrt(mean_square + norm_epsilon), (owners, 128))
 
@@ -527,11 +545,6 @@
 
         @pl.when(jnp.logical_not(f == t))
         def _(copy=copy):
-            copy.wait_send()
-
-    @pl.when(at_home)
-    def _():
-        for copy in scaled_out:
             copy.wait_send()
 
 
@@ -554,7 +567,7 @@
     seq_len, width = text_embeds.shape
     vtok, piece = vision_tokens.shape
     rows_per, columns = w_query.shape
-    vocab = lm_head.shape[1]
+    words = -(-lm_head.shape[1] // (16 * seq_count)) * 16
     owners = groups // seq_count
     local_heads = columns // HD
     heads = local_heads * seq_count
@@ -563,7 +576,7 @@
     smem = pl.BlockSpec(memory_space=pltpu.SMEM)
     any_space = pl.BlockSpec(memory_space=pl.ANY)
     phases = 12
-    links = max(groups, owners * seq_count)
+    links = groups * seq_count
     rms, best = pl.pallas_call(
         functools.partial(fused_kernel, groups, seq_count, capacity),
         out_shape=[jax.ShapeDtypeStruct((owners, 128), F32)] * 2,
@@ -576,7 +589,7 @@
             pltpu.VMEM((rows_per, columns), BF16),
             pltpu.VMEM((rows_per, columns), BF16),
             pltpu.VMEM((columns, rows_per), BF16),
-            pltpu.VMEM((piece, vocab), BF16),
+            pltpu.VMEM((words, width), BF16),
             pltpu.VMEM((seq_len, piece), BF16),
             pltpu.VMEM((heads, piece), F32),
             pltpu.VMEM((groups, 2, rows_per), F32),
@@ -585,27 +598,27 @@
             pltpu.VMEM((groups, capacity, piece), BF16),
             pltpu.VMEM((groups, 1, 128), F32),
             pltpu.VMEM((groups, 1, 128), F32),
-            pltpu.VMEM((groups, columns), F32),
-            pltpu.VMEM((groups, groups, columns), F32),
+            pltpu.VMEM((2 * groups, columns // 2), BF16),
+            pltpu.VMEM((groups, 2 * groups, columns // 2), BF16),
             pltpu.VMEM((groups, local_heads, rows_per), F32),
             pltpu.VMEM((owners, seq_count, local_heads, rows_per), F32),
-            pltpu.VMEM((seq_count, heads + 8, seq_len), F32),
+            pltpu.VMEM((seq_count, heads, seq_len), F32),
+            pltpu.VMEM((seq_count, 8, seq_len), F32),
             pltpu.VMEM((owners, seq_count, local_heads, rows_per), F32),
             pltpu.VMEM((groups, local_heads, rows_per), F32),
-            pltpu.VMEM((groups, columns), F32),
-            pltpu.VMEM((groups, groups, columns), F32),
+            pltpu.VMEM((2 * groups, columns // 2), BF16),
+            pltpu.VMEM((groups, 2 * groups, columns // 2), BF16),
             pltpu.VMEM((seq_count, groups, rows_per), F32),
             pltpu.VMEM((2 * groups, rows_per // 2), BF16),
-            pltpu.VMEM((owners, 2 * groups, rows_per // 2), BF16),
-            pltpu.VMEM((seq_count, owners, vocab), F32),
-            pltpu.VMEM((seq_count, owners, vocab), F32),
-            pltpu.VMEM((groups, owners, 128), F32),
+            pltpu.VMEM((groups, 2 * groups, rows_per // 2), BF16),
+            pltpu.VMEM((seq_count, owners, 128), F32),
+            pltpu.VMEM((groups * seq_count, owners, 128), F32),
             pltpu.SemaphoreType.DMA((7,)),
             pltpu.SemaphoreType.DMA((phases, links)),
             pltpu.SemaphoreType.DMA((phases, links)),
         ],
         compiler_params=pltpu.CompilerParams(
-            collective_id=0, has_side_effects=True, vmem_limit_bytes=48 * 2**20
+            collective_id=0, has_side_effects=True, vmem_limit_bytes=56 * 2**20
         ),
         name="fused",
     )(
@@ -620,7 +633,7 @@
         w_key,
         w_value,
         w_out,
-        lm_head,
+        lm_head.T,
     )
     return rms[:, 0], best[:, 0]
 

time: 105 us -> 64.7 us (0.62)
  local copies, waits for them, and re-layouts: 43.5 us -> 1.35 us
  Pallas kernels: 58.2 us -> 61 us
    unnamed x17 -> x0, local copies, waits for them, and re-layouts: 42.8 us -> none
    pallas_call x1, Pallas kernels: 58.2 us -> 61 us  [fused(): pl.pallas_call(functools.partial(fused_kernel, groups, seq_count, capacit...]
where the time goes in v3:
time: 64.7 us; the launch traced here: 64.3 us
  Pallas kernels  61 us (94%)
  between operations  1.93 us (3%)
  local copies, waits for them, and re-layouts  1.35 us (2%)
    pallas_call x1, Pallas kernels, fused(): pl.pallas_call(functools.partial(fused_kernel, groups, seq_count, capacit...  61 us
    slice x1, local copies, waits for them, and re-layouts, fused(): return (rms[:, 0], best[:, 0])  1.35 us

profile of v3, /device:TPU:0, one launch (start us, length us, event | category | flops | bytes accessed | tf_op | source)
XLA Modules:
  0.0 64.3 jit_solution(4530035166030046536)
XLA Ops:
  1.9 61.0 %fused.1 = (f32[2,128]{1,0:T(2,128)}, f32[2,128]{1,0:T(2,128)}) custom-call(s32[1,128]{1,0:T(1,128)} %bitcast.7, s32[1]{0:T(128)S(6)} %copy.14.start, s32[1]{0:T(128)S(6)} %copy.15.lengths, f32[1,4096]{1,0:T(1,128)} %bitcast.5, f32[1,4096]{1,0:T(1,128)} %bitcast.6, bf16[280,4096]{1,0:T(8,128)(2,1)} %text_hbm.1, bf16[128,1024]{1,0:T(8,128)(2,1)} %vision_hbm.1, ...), custom_call_target="tpu_custom_call" | custom-call | tf_op jit(solution)/shard_map/fused/pallas_call | solution.py:580
  63.0 1.3 %slice_reduce_fusion = (f32[2]{0:T(128)}, f32[2]{0:T(128)}) fusion(f32[2,128]{1,0:T(2,128)} %get-tuple-element.5, f32[2,128]{1,0:T(2,128)} %get-tuple-element.4), kind=kLoop, calls=%fused_computation | loop fusion | bytes 32 | tf_op jit(solution)/shard_map/slice | solution.py:638
